TPU v7x, 32 devices: a whole 2x2x4 slice. The times are simulated.
32 devices in a mesh: section: 4 (over x, core), ctx: 2 (over y), tp: 4 (over z).
Axes of the slice: x: 2, y: 2, z: 4, core: 2. Of those that a mesh axis runs over, the one named last changes fastest.
Arguments:
- stretch_order: int32 [2, 2], replicated, may hold values from 0 to 3, as said below
- queries: bfloat16 [4, 1024, 2048], P('section', 'ctx', 'tp'), may hold values from -60 to 60
- key_rows: bfloat16 [4, 1024, 512], P('section', 'ctx', 'tp'), may hold values from -7 to 7
- value_rows: bfloat16 [4, 1024, 512], P('section', 'ctx', 'tp'), may hold values from -5 to 5
- out_grad: bfloat16 [4, 1024, 4096], P('section', ('ctx', 'tp')), may hold values from -6 to 6
- query_weight: bfloat16 [4, 4096, 2048], P('section', None, 'tp'), may hold values from -0.09375 to 0.09375
- key_weight: bfloat16 [4, 4096, 512], P('section', None, 'tp'), may hold values from -0.09375 to 0.09375
- value_weight: bfloat16 [4, 4096, 512], P('section', None, 'tp'), may hold values from -0.09375 to 0.09375
- output_weight: bfloat16 [4, 2048, 4096], P('section', 'tp'), may hold values from -0.125 to 0.125
Outputs:
- sent_grad: bfloat16 [4, 1024, 4096], P('section', ('ctx', 'tp'))
- key_grad: bfloat16 [4, 1024, 512], P('section', 'ctx', 'tp')
- value_grad: bfloat16 [4, 1024, 512], P('section', 'ctx', 'tp')
Inputs may be any that keep to these rules, and one draw needn't show every extreme that they name: `stretch_order`: row c lists the ids of the two blocks of 256 consecutive positions stored, in that order, at ctx index c; the two ids of a row sum to 3 and every id occurs once.
All inputs are finite; a program needn't handle non-finite values.
Results may differ from a plain program's by a relative error of at most 0.015.
Values may be sent and summed in bfloat16 or wider, within the bound.
A program may use at most 128 MiB of HBM per device.

v0:
```python
import jax
import jax.numpy as jnp
from jax import lax
from jax.sharding import PartitionSpec as P

HD = 128
HQ = 16
KV = 4


NEG_LARGE = -1e30


def shifted(block, axis, distance):
    devices = range(lax.axis_size(axis))
    route = [((i - distance) % len(devices), i) for i in devices]
    return lax.ppermute(block, axis, route)


def contract_last(lhs, rhs):
    return lax.dot_general(lhs, rhs, (((1,), (1,)), ((), ())), preferred_element_type=jnp.float32)


def key_positions(flat_order, offset, row_count, block_len):
    row_ids = offset + jnp.arange(row_count, dtype=jnp.int32)
    owner = row_ids // block_len
    table = jnp.arange(flat_order.shape[0], dtype=jnp.int32)
    picked = jnp.sum(jnp.where(owner[:, None] == table[None, :], flat_order[None, :], 0), axis=1)
    return picked * block_len + row_ids % block_len


def block_scores(query_blk, grad_blk, key_blk, value_blk, score_scale):
    scores = (
        jnp.einsum("qghe,kge->ghqk", query_blk, key_blk, preferred_element_type=jnp.float32)
        * score_scale
    )
    grad_probs = jnp.einsum(
        "qghe,kge->ghqk", grad_blk, value_blk, preferred_element_type=jnp.float32
    )
    return (scores, grad_probs)


def stats_update(running, query_blk, grad_blk, query_pos, key_blk, value_blk, key_pos, score_scale):
    run_max, run_sum, run_dot = running
    scores, grad_probs = block_scores(query_blk, grad_blk, key_blk, value_blk, score_scale)
    visible = key_pos[None, :] <= query_pos[:, None]
    masked = jnp.where(visible, scores, NEG_LARGE)
    new_max = jnp.maximum(run_max, jnp.max(masked, axis=-1))
    weights = jnp.where(visible, jnp.exp(masked - new_max[..., None]), 0.0)
    new_sum = jnp.sum(weights, axis=-1)
    new_dot = jnp.sum(weights * grad_probs, axis=-1)
    return (new_max, new_sum, new_dot)


def block_grads(query_part, key_blk, value_blk, key_pos, score_scale):
    query_blk, grad_blk, query_pos, lse_blk, delta_blk = query_part
    scores, grad_probs = block_scores(query_blk, grad_blk, key_blk, value_blk, score_scale)
    visible = key_pos[None, :] <= query_pos[:, None]
    attn_probs = jnp.where(visible, jnp.exp(scores - lse_blk[..., None]), 0.0)
    dscore = attn_probs * (grad_probs - delta_blk[..., None])
    probs_low = attn_probs.astype(jnp.bfloat16)
    dscore_low = dscore.astype(jnp.bfloat16)
    results = []
    results.append(
        jnp.einsum("ghqk,kge->qghe", dscore_low, key_blk, preferred_element_type=jnp.float32)
        * score_scale
    )
    results.append(
        jnp.einsum("ghqk,qghe->kge", dscore_low, query_blk, preferred_element_type=jnp.float32)
        * score_scale
    )
    results.append(
        jnp.einsum("ghqk,qghe->kge", probs_low, grad_blk, preferred_element_type=jnp.float32)
    )
    return tuple(results)


def guarded(query_part, key_blk, value_blk, key_pos, score_scale, zero_like):

    def guarded_active(operands):
        return block_grads(query_part, operands[0], operands[1], operands[2], score_scale)

    def skipped(operands):
        return zero_like

    return lax.cond(
        jnp.min(key_pos) <= jnp.max(query_part[2]),
        guarded_active,
        skipped,
        (key_blk, value_blk, key_pos),
    )


def per_device(
    stretch_order,
    queries,
    key_rows,
    value_rows,
    out_grad,
    query_weight,
    key_weight,
    value_weight,
    output_weight,
):
    score_scale = HD ** (-0.5)
    group_len = HQ // KV
    query_mat = queries[0]
    key_mat = key_rows[0]
    value_mat = value_rows[0]
    tok_dev = query_mat.shape[0]
    block_len = tok_dev // 2
    kv_dev = key_mat.shape[1] // HD
    block_total = 2 * lax.axis_size("ctx")
    flat_order = stretch_order.reshape(-1)
    own_ids = lax.dynamic_slice_in_dim(flat_order, 2 * lax.axis_index("ctx"), 2, 0)
    out_weight = output_weight[0]
    attn_grad = contract_last(
        lax.all_gather(out_grad[0], "tp", axis=0, tiled=True), out_weight
    ).astype(jnp.bfloat16)
    query_four = query_mat.reshape(tok_dev, kv_dev, group_len, HD)
    grad_four = attn_grad.reshape(tok_dev, kv_dev, group_len, HD)
    local_pos = jnp.arange(block_len, dtype=jnp.int32)
    query_halves = []
    for half_idx in range(2):
        query_halves.append(
            (
                query_four[half_idx * block_len : (half_idx + 1) * block_len],
                grad_four[half_idx * block_len : (half_idx + 1) * block_len],
                own_ids[half_idx] * block_len + local_pos,
            )
        )
    stat_shape = (kv_dev, group_len, block_len)
    init_one = (
        jnp.full(stat_shape, NEG_LARGE, jnp.float32),
        jnp.zeros(stat_shape, jnp.float32),
        jnp.zeros(stat_shape, jnp.float32),
    )
    init_stats = (init_one, init_one)
    keys_all, values_all = (
        lax.all_gather(key_mat, "ctx", axis=0, tiled=True),
        lax.all_gather(value_mat, "ctx", axis=0, tiled=True),
    )
    keys_three = keys_all.reshape(-1, kv_dev, HD)
    values_three = values_all.reshape(-1, kv_dev, HD)
    seq_rows = keys_three.shape[0]
    pieces_in = (
        lax.all_gather(key_mat, "ctx", axis=0, tiled=True),
        lax.all_gather(value_mat, "ctx", axis=0, tiled=True),
    )
    row_count = pieces_in[0].shape[0]
    key_blk = pieces_in[0].reshape(row_count, kv_dev, HD)
    value_blk = pieces_in[1].reshape(row_count, kv_dev, HD)
    key_pos = key_positions(flat_order, jnp.int32(0), row_count, block_len)
    updated = []
    for stats_half_idx in range(2):
        query_blk, grad_blk, query_pos = query_halves[stats_half_idx]

        def stats_active(state):
            return stats_update(
                state, query_blk, grad_blk, query_pos, key_blk, value_blk, key_pos, score_scale
            )

        def unchanged(state):
            return state

        updated.append(
            lax.cond(
                jnp.min(key_pos) <= jnp.max(query_pos),
                stats_active,
                unchanged,
                init_stats[stats_half_idx],
            )
        )
    running = tuple(updated)
    full_parts = []
    for half_idx in range(2):
        run_max, run_sum, run_dot = running[half_idx]
        lse_blk = run_max + jnp.log(run_sum)
        delta_blk = run_dot / run_sum
        full_parts.append(query_halves[half_idx] + (lse_blk, delta_blk))
    zero_query = jnp.zeros((block_len, kv_dev, group_len, HD), jnp.float32)
    zero_keys = jnp.zeros((block_len, kv_dev, HD), jnp.float32)

    def grad_step(block_idx, state):
        query_sums, key_sums, value_sums = state
        offset = block_idx * block_len
        key_blk = lax.dynamic_slice_in_dim(keys_three, offset, block_len, 0)
        value_blk = lax.dynamic_slice_in_dim(values_three, offset, block_len, 0)
        key_pos = key_positions(flat_order, offset, block_len, block_len)
        key_add = zero_keys
        value_add = zero_keys
        new_query = []
        for half_idx in range(2):
            part_query, part_key, part_value = guarded(
                full_parts[half_idx],
                key_blk,
                value_blk,
                key_pos,
                score_scale,
                (zero_query, zero_keys, zero_keys),
            )
            new_query.append(query_sums[half_idx] + part_query)
            key_add = key_add + part_key
            value_add = value_add + part_value
        key_sums = lax.dynamic_update_slice_in_dim(
            key_sums, lax.dynamic_slice_in_dim(key_sums, offset, block_len, 0) + key_add, offset, 0
        )
        value_sums = lax.dynamic_update_slice_in_dim(
            value_sums,
            lax.dynamic_slice_in_dim(value_sums, offset, block_len, 0) + value_add,
            offset,
            0,
        )
        return (tuple(new_query), key_sums, value_sums)

    zero_full = jnp.zeros((seq_rows, kv_dev, HD), jnp.float32)
    query_sums, key_sums, value_sums = lax.fori_loop(
        0, block_total, grad_step, ((zero_query, zero_query), zero_full, zero_full)
    )
    key_own, value_own = (
        lax.psum_scatter(
            key_sums.astype(jnp.bfloat16), "ctx", scatter_dimension=0, tiled=True
        ).astype(jnp.float32),
        lax.psum_scatter(
            value_sums.astype(jnp.bfloat16), "ctx", scatter_dimension=0, tiled=True
        ).astype(jnp.float32),
    )
    query_grad = (
        jnp.concatenate(query_sums, axis=0)
        .reshape(tok_dev, kv_dev * group_len * HD)
        .astype(jnp.bfloat16)
    )
    key_grad = key_own.reshape(tok_dev, kv_dev * HD).astype(jnp.bfloat16)
    value_grad = value_own.reshape(tok_dev, kv_dev * HD).astype(jnp.bfloat16)
    query_mixer = query_weight[0]
    key_mixer = key_weight[0]
    value_mixer = value_weight[0]
    summed = contract_last(query_grad, query_mixer)
    summed = summed + contract_last(key_grad, key_mixer)
    summed = summed + contract_last(value_grad, value_mixer)
    input_grad = lax.psum_scatter(
        summed.astype(jnp.bfloat16), "tp", scatter_dimension=0, tiled=True
    )
    sent_grad = shifted(input_grad, "section", -1)
    return (sent_grad[None], key_grad[None], value_grad[None])


def solution(mesh):
    placed = (
        P(),
        P("section", "ctx", "tp"),
        P("section", "ctx", "tp"),
        P("section", "ctx", "tp"),
        P("section", ("ctx", "tp"), None),
        P("section", None, "tp"),
        P("section", None, "tp"),
        P("section", None, "tp"),
        P("section", "tp", None),
    )
    return jax.shard_map(
        per_device,
        mesh=mesh,
        in_specs=placed,
        out_specs=(
            P("section", ("ctx", "tp"), None),
            P("section", "ctx", "tp"),
            P("section", "ctx", "tp"),
        ),
        check_vma=False,
    )
```

profile of v0, /device:TPU:9, one launch (start us, length us, event | category | flops | bytes accessed | tf_op | source)
XLA Modules:
  0.0 298.5 jit_solution(8448547161504509978)
XLA Ops:
  19.1 5.1 %all-gather = bf16[1,1024,128]{2,1,0:T(8,128)(2,1)} all-gather(bf16[1,512,128]{2,1,0:T(8,128)(2,1)S(1)} %copy-done.4), channel_id=2, replica_groups=mesh['section'=4,'ctx'=2,'tp'=4] {'ctx'}, dimensions={1}, use_global_device_ids=true | all-gather | bytes 393216 | tf_op jit(solution)/shard_map/all_gather | solution.py:140
  24.3 4.9 %all-gather.1 = bf16[1,1024,128]{2,1,0:T(8,128)(2,1)} all-gather(bf16[1,512,128]{2,1,0:T(8,128)(2,1)S(1)} %copy-done.5), channel_id=3, replica_groups=mesh['section'=4,'ctx'=2,'tp'=4] {'ctx'}, dimensions={1}, use_global_device_ids=true | all-gather | bytes 393216 | tf_op jit(solution)/shard_map/all_gather | solution.py:141
  29.2 59.9 %all-gather.5.cloned.1.call-done = bf16[1,512,4096]{2,1,0:T(8,128)(2,1)} async-done(((bf16[1,128,4096]{2,1,0:T(8,128)(2,1)}), bf16[1,512,4096]{2,1,0:T(8,128)(2,1)}) %all-gather.5.cloned.1.call-update) | async-done | bytes 4194320 | tf_op jit(solution)/shard_map/all_gather | solution.py:118
  89.0 5.8 %fusion.69 = bf16[512,512]{0,1:T(8,128)(2,1)S(1)} fusion(bf16[1,512,4096]{2,1,0:T(8,128)(2,1)} %param.27, bf16[1,512,4096]{2,1,0:T(8,128)(2,1)} %all-gather.5.cloned.1.call-done), kind=kOutput, calls=%fused_computation.111 | convolution fusion | flops 2147745792 | bytes 8912896 | tf_op jit(solution)/shard_map/dot_general | solution.py:21
  95.3 5.5 %conditional.5 = (f32[1,4,256]{2,1,0:T(4,128)S(1)}, f32[1,4,256]{2,1,0:T(4,128)S(1)}, f32[1,4,256]{2,1,0:T(4,128)S(1)}) conditional(s32[]{:T(128)} %convert_element_type.87, () %tuple.80, (s32[1024]{0:T(1024)S(1)}, s32[256]{0:T(256)S(1)}, bf16[1024,1,128]{2,0,1:T(8,128)(2,1)}, bf16[256,1,4,128]{0,3,2,1:T(8,128)(2,1)S(1)}, ...), branch_computations={%region_9.10_spmd, %region_10.14_spmd} | conditional | flops 551812096 | bytes 14734360 | solution.py:167
  97.3 2.4 fusion.13
  100.7 5.6 %conditional.4 = (f32[1,4,256]{2,1,0:T(4,128)S(1)}, f32[1,4,256]{2,1,0:T(4,128)S(1)}, f32[1,4,256]{2,1,0:T(4,128)S(1)}) conditional(s32[]{:T(128)} %convert_element_type.85, () %tuple.78, (s32[1024]{0:T(1024)S(1)}, s32[256]{0:T(256)S(1)}, bf16[1024,1,128]{2,0,1:T(8,128)(2,1)}, bf16[256,1,4,128]{0,3,2,1:T(8,128)(2,1)S(1)}, ...), branch_computations={%region_3.4_spmd, %region_4.8_spmd} | conditional | flops 551812096 | bytes 14734360 | solution.py:167
  102.7 2.4 fusion.4
  108.1 52.3 %while.23 = (s32[]{:T(128)}, f32[256,1,4,128]{3,0,2,1:T(8,128)}, f32[256,1,4,128]{3,0,2,1:T(8,128)S(1)}, f32[1024,1,128]{2,0,1:T(8,128)}, f32[1024,1,128]{2,0,1:...) while((s32[]{:T(128)}, f32[256,1,4,128]{3,0,2,1:T(8,128)}, ...), condition=%wide.wide.region_21.22_spmd.clone, body=%wide.wide.region_14.21_spmd.clone.sunk | while | flops 675884032 | bytes 19824224 | solution.py:217
  113.2 2.7 conditional.13
  124.5 3.6 %conditional.12 = (f32[256,1,4,128]{3,0,2,1:T(8,128)S(1)}, f32[256,1,128]{2,0,1:T(8,128)S(1)}, f32[256,1,128]{2,0,1:T(8,128)S(1)}) conditional(s32[]{:T(128)} %convert_element_type.117, () %tuple.145, (s32[256]{0:T(256)S(1)}, s32[]{:T(128)}, bf16[256,1,128]{2,0,1:T(8,128)(2,1)S(1)}, bf16[256,1,4,128]{3,0,2,1:T(8,128)(2,1)}, ...), branch_computations={%region_19.19_spmd, %region_20.20_spmd} | conditional | flops 337608960 | bytes 6893596 | solution.py:86
  128.1 2.7 conditional.13
  131.5 2.2 select_add_fusion.4
  140.6 2.7 conditional.13
  144.0 2.2 select_add_fusion.4
  153.0 2.7 conditional.13
  156.4 2.2 select_add_fusion.4
  165.4 7.8 %fusion.64 = f32[512,4096]{1,0:T(8,128)} fusion(bf16[1,4096,512]{2,1,0:T(8,128)(2,1)} %param.24, bf16[256,512]{0,1:T(8,128)(2,1)S(1)} %bitcast.285, bf16[256,512]{0,1:T(8,128)(2,1)S(1)} %bitcast.284), kind=kOutput, calls=%fused_computation.106 | convolution fusion | flops 2148532224 | bytes 13107200 | tf_op jit(solution)/shard_map/dot_general | solution.py:21
  173.2 2.8 reduce-scatter.4.cloned.1.call-done
  176.0 5.4 %fusion.75 = f32[512,4096]{1,0:T(8,128)} fusion(bf16[1,4096,128]{2,1,0:T(8,128)(2,1)S(1)} %copy-done, bf16[512,1,128]{2,0,1:T(8,128)(2,1)} %reduce-scatter.4.cloned.1.call-done), kind=kOutput, calls=%fused_computation.113 | convolution fusion | flops 536870912 | bytes 9568256 | tf_op jit(solution)/shard_map/dot_general | solution.py:21
  181.4 9.2 %reduce-scatter.6.cloned.1.call-done = bf16[512,1,128]{2,0,1:T(8,128)(2,1)} async-done(((bf16[1024,1,128]{2,0,1:T(8,128)(2,1)}), bf16[512,1,128]{2,0,1:T(8,128)(2,1)}) %reduce-scatter.6.cloned.1.call-update) | async-done | bytes 131088 | tf_op jit(solution)/shard_map/reduce_scatter | solution.py:224
  190.6 9.0 %add_convert_fusion = bf16[512,4096]{1,0:T(8,128)(2,1)} fusion(f32[512,4096]{1,0:T(8,128)} %fusion.64, f32[512,4096]{1,0:T(8,128)} %fusion.75, bf16[1,4096,128]{2,1,0:T(8,128)(2,1)S(1)} %copy-done.3, bf16[512,1,128]{2,0,1:T(8,128)(2,1)} %reduce-scatter.6.cloned.1.call-done), kind=kOutput, calls=%fused_computation.105 | convolution fusion | flops 543162368 | bytes 22151168 | tf_op jit(solution)/shard_map/dot_general | solution.py:21
  199.6 77.0 %reduce-scatter.8.cloned.1.call-done = bf16[128,4096]{1,0:T(8,128)(2,1)} async-done(((bf16[512,4096]{1,0:T(8,128)(2,1)}), bf16[128,4096]{1,0:T(8,128)(2,1)}) %reduce-scatter.8.cloned.1.call-update) | async-done | bytes 1048592 | tf_op jit(solution)/shard_map/reduce_scatter | solution.py:241
  277.2 13.8 %collective-permute-done = bf16[128,4096]{1,0:T(8,128)(2,1)S(1)} collective-permute-done((bf16[128,4096]{1,0:T(8,128)(2,1)}, bf16[128,4096]{1,0:T(8,128)(2,1)S(1)}, u32[]{:S(2)}, u32[]{:S(2)}) %collective-permute-start) | collective-permute-done | bytes 1048608 | tf_op jit(solution)/shard_map/ppermute | solution.py:17
  (151 shorter events, 57.9 us)
Async XLA Ops:
  7.2 168.8 %copy-start = (bf16[1,4096,128]{2,1,0:T(8,128)(2,1)S(1)}, bf16[1,4096,128]{2,1,0:T(8,128)(2,1)}, u32[]{:S(2)}) copy-start(bf16[1,4096,128]{2,1,0:T(8,128)(2,1)} %param.25) | copy-start | bytes 3145732
  7.2 11.9 %copy-start.4 = (bf16[1,512,128]{2,1,0:T(8,128)(2,1)S(1)}, bf16[1,512,128]{2,1,0:T(8,128)(2,1)}, u32[]{:S(2)}) copy-start(bf16[1,512,128]{2,1,0:T(8,128)(2,1)} %param.21) | copy-start | bytes 393220
  7.2 17.1 %copy-start.5 = (bf16[1,512,128]{2,1,0:T(8,128)(2,1)S(1)}, bf16[1,512,128]{2,1,0:T(8,128)(2,1)}, u32[]{:S(2)}) copy-start(bf16[1,512,128]{2,1,0:T(8,128)(2,1)} %param.22) | copy-start | bytes 393220
  7.2 81.8 %all-gather.5.cloned.1.call-start = ((), (), s32[]{:S(2)}) async-start(), calls=%async_computation.6 | async-start | bytes 5242880 | tf_op jit(solution)/shard_map/all_gather | solution.py:118
  7.9 168.1 %reduce-scatter.4.cloned.1.call-start = ((), (), s32[]{:S(2)}) async-start(), calls=%async_computation.3 | async-start | bytes 393216 | tf_op jit(solution)/shard_map/reduce_scatter | solution.py:221
  113.2 2.1 copy-start.2
  115.9 0.7 copy-start.1
  128.1 2.1 copy-start.2
  130.9 0.7 copy-start.1
  140.6 2.1 copy-start.2
  143.3 0.7 copy-start.1
  153.0 2.1 copy-start.2
  155.8 0.7 copy-start.1
  162.2 28.4 %reduce-scatter.6.cloned.1.call-start = ((), (), s32[]{:S(2)}) async-start(), calls=%async_computation.4 | async-start | bytes 393216 | tf_op jit(solution)/shard_map/reduce_scatter | solution.py:224
  165.4 111.2 %reduce-scatter.8.cloned.1.call-start = ((), (), s32[]{:S(2)}) async-start(), calls=%async_computation.5 | async-start | bytes 5242880 | tf_op jit(solution)/shard_map/reduce_scatter | solution.py:241
  173.2 17.4 %copy-start.3 = (bf16[1,4096,128]{2,1,0:T(8,128)(2,1)S(1)}, bf16[1,4096,128]{2,1,0:T(8,128)(2,1)}, u32[]{:S(2)}) copy-start(bf16[1,4096,128]{2,1,0:T(8,128)(2,1)} %param.26) | copy-start | bytes 3145732
  276.6 14.4 %collective-permute-start = (bf16[128,4096]{1,0:T(8,128)(2,1)}, bf16[128,4096]{1,0:T(8,128)(2,1)S(1)}, u32[]{:S(2)}, u32[]{:S(2)}) collective-permute-start(bf16[128,4096]{1,0:T(8,128)(2,1)} %reduce-scatter.8.cloned.1.call-done), channel_id=1, source_target_pairs={{8,0},{16,8},{24,16},{0,24},{9,1},{17,9},{25,17},{1,25},{10,2},{18... | collective-permute-start | bytes 3145736 | tf_op jit(solution)/shard_map/ppermute | solution.py:17
Sparse Core Ops, SparseCore 0:
  9.6 79.3 all-gather.4
  162.3 13.6 reduce-scatter.3
  178.9 11.6 reduce-scatter.5
  199.7 76.8 reduce-scatter.7
where the time goes:
time: 302 us; the launch traced here: 299 us
  waiting for transfers between devices  163 us (54%)
  matrix products  49.9 us (17%)
  other arithmetic  26.4 us (9%)
  local copies, waits for them, and re-layouts  19.2 us (6%)
  between operations  17.7 us (6%)
  loops' own time  11.1 us (4%)
  blocking collectives  10 us (3%)
    reduce_scatter x1, waiting for transfers between devices, per_device(): lax.psum_scatter(summed.astype(jnp.bfloat16), 'tp', scatter_dimension=0,...  77 us
    all_gather x1, waiting for transfers between devices, per_device(): lax.all_gather(out_grad[0], 'tp', axis=0, tiled=True)  59.9 us
    dot_general x4, matrix products, contract_last(): lax.dot_general(lhs, rhs, (((1,), (1,)), ((), ())), preferred_element_typ...  28 us
    ppermute x1, waiting for transfers between devices, shifted(): return lax.ppermute(block, axis, route)  13.8 us
    another operation x1, loops' own time, per_device(): lax.fori_loop(0, block_total, grad_step, ((zero_query, zero_query), zero_...  10.4 us
    dot_general x7, matrix products, block_scores(): jnp.einsum('qghe,kge->ghqk', query_blk, key_blk, preferred_element_type=j...  10.1 us
    reduce_scatter x1, waiting for transfers between devices, per_device(): lax.psum_scatter(value_sums.astype(jnp.bfloat16), 'ctx', scatter_dimensio...  9.23 us
    add x4, other arithmetic, grad_step(): new_query.append(query_sums[half_idx] + part_query)  7.66 us
  transfers between devices with their start and end apart: 5, of which 5 were waited for; matrix products, arithmetic and copies ran while one was open for 8% of the time, Pallas kernels for 0%

commit v1 on v0

v1 whole, which is shorter than its diff:
```python
import functools

import jax
import jax.numpy as jnp
from jax import lax
from jax.experimental import pallas as pl
from jax.experimental.pallas import tpu as pltpu
from jax.sharding import PartitionSpec as P

HD = 128
BLOCK = 256
MASKED = -1e30
LOG2E = 1.4426950408889634
CHUNK = 512
MESH = pl.DeviceIdType.MESH
VMEM = pl.BlockSpec(memory_space=pltpu.VMEM)
SMEM = pl.BlockSpec(memory_space=pltpu.SMEM)
LIMIT = 56 * 1024 * 1024


def dot_nt(lhs, rhs):
    return lax.dot_general(lhs, rhs, (((1,), (1,)), ((), ())), preferred_element_type=jnp.float32)


def dot_nn(lhs, rhs):
    return jnp.dot(lhs, rhs, preferred_element_type=jnp.float32)


def greet(peers):
    barrier = pltpu.get_barrier_semaphore()
    for peer in peers:
        pl.semaphore_signal(barrier, inc=1, device_id=peer, device_id_type=MESH)
    pl.semaphore_wait(barrier, len(peers))


def gather_kernel(
    n_tp, n_ctx, og_ref, wo_ref, k_ref, v_ref, grad_ref, kall_ref, vall_ref,
    shards, og_send, og_recv, kv_send, kv_recv,
):
    me = lax.axis_index("tp")
    ctx = lax.axis_index("ctx")
    rows = og_ref.shape[0]
    tok = k_ref.shape[0]
    greet(
        [{"tp": lax.rem(me + i, n_tp)} for i in range(1, n_tp)]
        + [{"ctx": lax.rem(ctx + i, n_ctx)} for i in range(1, n_ctx)]
    )
    sent = []
    for i in range(1, n_tp):
        copy = pltpu.make_async_remote_copy(
            src_ref=og_ref, dst_ref=shards.at[i - 1], send_sem=og_send.at[i - 1],
            recv_sem=og_recv.at[i - 1], device_id={"tp": lax.rem(me + i, n_tp)},
            device_id_type=MESH,
        )
        copy.start()
        sent.append(copy)
    place = pl.ds(pl.multiple_of(ctx * tok, tok), tok)
    kv_sent = []
    for i in range(1, n_ctx):
        for which, (src, dst) in enumerate(((k_ref, kall_ref), (v_ref, vall_ref))):
            copy = pltpu.make_async_remote_copy(
                src_ref=src, dst_ref=dst.at[place], send_sem=kv_send.at[which, i - 1],
                recv_sem=kv_recv.at[which, i - 1], device_id={"ctx": lax.rem(ctx + i, n_ctx)},
                device_id_type=MESH,
            )
            copy.start()
            kv_sent.append(copy)
    kall_ref[place, :] = k_ref[...]
    vall_ref[place, :] = v_ref[...]

    def store(owner, block):
        at = pl.ds(pl.multiple_of(owner * rows, rows), rows)
        grad_ref[at, :] = dot_nt(block[...], wo_ref[...]).astype(grad_ref.dtype)

    store(me, og_ref)
    for i in range(1, n_tp):
        sent[i - 1].wait_recv()
        store(lax.rem(me - i + n_tp, n_tp), shards.at[i - 1])
    for i in range(1, n_ctx):
        source = lax.rem(ctx - i + n_ctx, n_ctx)
        at = pl.ds(pl.multiple_of(source * tok, tok), tok)
        for which, (src, dst) in enumerate(((k_ref, kall_ref), (v_ref, vall_ref))):
            pltpu.make_async_remote_copy(
                src_ref=src, dst_ref=dst.at[at], send_sem=kv_send.at[which, i - 1],
                recv_sem=kv_recv.at[which, i - 1], device_id={"ctx": lax.rem(ctx + i, n_ctx)},
                device_id_type=MESH,
            ).wait_recv()
    for copy in sent + kv_sent:
        copy.wait_send()


def attention_kernel(
    order_ref, q_ref, g_ref, k_ref, v_ref, dq_ref, dkv_ref, dk_acc, dv_acc, kt_ref
):
    ctx = lax.axis_index("ctx")
    blocks = k_ref.shape[0] // BLOCK
    heads = q_ref.shape[1] // HD
    scale = HD ** (-0.5)
    for b in range(blocks):
        at = slice(b * BLOCK, (b + 1) * BLOCK)
        kt_ref[:, at] = k_ref[at, :].astype(jnp.float32).T.astype(jnp.bfloat16)
    dk_acc[...] = jnp.zeros_like(dk_acc)
    dv_acc[...] = jnp.zeros_like(dv_acc)
    shape = (BLOCK, BLOCK)
    lead = lax.broadcasted_iota(jnp.int32, shape, 0) - lax.broadcasted_iota(jnp.int32, shape, 1)

    def step(i, _):
        half, head = i // heads, lax.rem(i, heads)
        rows = pl.ds(pl.multiple_of(half * BLOCK, BLOCK), BLOCK)
        cols = pl.ds(pl.multiple_of(head * HD, HD), HD)
        q = q_ref[rows, cols]
        g = g_ref[rows, cols]
        query_id = order_ref[ctx, half]
        scores = []
        for b in range(blocks):
            ahead = (query_id - order_ref[b // 2, b % 2]) * BLOCK
            s = dot_nt(k_ref[b * BLOCK:(b + 1) * BLOCK, :], q)
            scores.append(jnp.where(lead <= ahead, s, MASKED))
        top = functools.reduce(
            jnp.maximum, [jnp.max(s, axis=0, keepdims=True) for s in scores]
        )
        weights = [jnp.exp2((s - top) * (scale * LOG2E)) for s in scores]
        gps = [dot_nt(v_ref[b * BLOCK:(b + 1) * BLOCK, :], g) for b in range(blocks)]
        total = sum(jnp.sum(w, axis=0, keepdims=True) for w in weights)
        dots = sum(jnp.sum(w * p, axis=0, keepdims=True) for w, p in zip(weights, gps))
        inv = 1.0 / total
        delta = dots * inv
        dqt = jnp.zeros((HD, BLOCK), jnp.float32)
        for b in range(blocks):
            at = slice(b * BLOCK, (b + 1) * BLOCK)
            probs = weights[b] * inv
            ds = (probs * (gps[b] - delta)).astype(jnp.bfloat16)
            dv_acc[at, :] += dot_nn(probs.astype(jnp.bfloat16), g)
            dk_acc[at, :] += dot_nn(ds, q)
            dqt += dot_nn(kt_ref[:, at], ds)
        dq_ref[rows, cols] = (dqt * scale).T.astype(dq_ref.dtype)
        return 0

    lax.fori_loop(0, 2 * heads, step, 0)
    dkv_ref[0] = (dk_acc[...] * scale).astype(dkv_ref.dtype)
    dkv_ref[1] = dv_acc[...].astype(dkv_ref.dtype)


def scatter_kernel(
    n_tp, n_ctx, n_sec, dq_ref, dkv_ref, wq_ref, wk_ref, wv_ref, out_ref, kg_ref, vg_ref,
    parts, right_in, right_out, left_in, left_out, relay,
    part_send, part_recv, right_send, right_recv, left_send, left_recv, relay_send, relay_recv,
):
    me = lax.axis_index("tp")
    ctx = lax.axis_index("ctx")
    sec = lax.axis_index("section")
    tok = kg_ref.shape[0]
    rows = out_ref.shape[0]
    chunks = out_ref.shape[1] // CHUNK
    before = lax.rem(sec + n_sec - 1, n_sec)
    greet(
        [{"tp": lax.rem(me + i, n_tp)} for i in range(1, n_tp)]
        + [{"ctx": lax.rem(ctx + i, n_ctx)} for i in range(1, n_ctx)]
        + [{"section": before}, {"section": lax.rem(sec + 1, n_sec)}]
    )
    part_sent = []
    for i in range(1, n_ctx):
        peer = lax.rem(ctx + i, n_ctx)
        copy = pltpu.make_async_remote_copy(
            src_ref=dkv_ref.at[:, pl.ds(pl.multiple_of(peer * tok, tok), tok)],
            dst_ref=parts.at[i - 1], send_sem=part_send.at[i - 1],
            recv_sem=part_recv.at[i - 1], device_id={"ctx": peer}, device_id_type=MESH,
        )
        copy.start()
        part_sent.append(copy)
    mine = pl.ds(pl.multiple_of(ctx * tok, tok), tok)
    kg = dkv_ref[0, mine, :].astype(jnp.float32)
    vg = dkv_ref[1, mine, :].astype(jnp.float32)
    for i in range(1, n_ctx):
        part_sent[i - 1].wait_recv()
        kg += parts[i - 1, 0].astype(jnp.float32)
        vg += parts[i - 1, 1].astype(jnp.float32)
    kg_ref[...] = kg.astype(kg_ref.dtype)
    vg_ref[...] = vg.astype(vg_ref.dtype)

    def term(block, c):
        at = pl.ds(pl.multiple_of(block * rows, rows), rows)
        cols = pl.ds(pl.multiple_of(c * CHUNK, CHUNK), CHUNK)
        out = dot_nt(dq_ref[at, :], wq_ref[cols, :])
        out += dot_nt(kg_ref[at, :], wk_ref[cols, :])
        out += dot_nt(vg_ref[at, :], wv_ref[cols, :])
        return out

    def right_copy(block, c):
        return pltpu.make_async_remote_copy(
            src_ref=right_out.at[block, c], dst_ref=right_in.at[block, c],
            send_sem=right_send.at[block, c], recv_sem=right_recv.at[block, c],
            device_id={"tp": lax.rem(me + 1, n_tp)}, device_id_type=MESH,
        )

    def left_copy(block, c):
        return pltpu.make_async_remote_copy(
            src_ref=left_out.at[block, c], dst_ref=left_in.at[block, c],
            send_sem=left_send.at[block, c], recv_sem=left_recv.at[block, c],
            device_id={"tp": lax.rem(me + n_tp - 1, n_tp)}, device_id_type=MESH,
        )

    def relay_copy(c):
        cols = pl.ds(pl.multiple_of(c * CHUNK, CHUNK), CHUNK)
        return pltpu.make_async_remote_copy(
            src_ref=relay.at[c], dst_ref=out_ref.at[:, cols],
            send_sem=relay_send.at[c], recv_sem=relay_recv.at[c],
            device_id={"section": before}, device_id_type=MESH,
        )

    def forward(make, inbox, outbox, has_source, block, c):
        outbox[block, c] = term(block, c).astype(outbox.dtype)

        @pl.when(has_source)
        def _():
            make(block, c).wait_recv()
            outbox[block, c] = (
                outbox[block, c].astype(jnp.float32) + inbox[block, c].astype(jnp.float32)
            ).astype(outbox.dtype)

        make(block, c).start()

    def forward_step(i, _):
        turn, c = i // chunks, lax.rem(i, chunks)
        far = n_tp - 1 - turn

        @pl.when(far > me)
        def _():
            forward(right_copy, right_in, right_out, me > 0, far, c)

        @pl.when(turn < me)
        def _():
            forward(left_copy, left_in, left_out, me < n_tp - 1, turn, c)

        return 0

    lax.fori_loop(0, (n_tp - 1) * chunks, forward_step, 0)

    def final_step(c, _):
        relay[c] = term(me, c).astype(relay.dtype)

        @pl.when(me > 0)
        def _():
            right_copy(me, c).wait_recv()
            relay[c] = (
                relay[c].astype(jnp.float32) + right_in[me, c].astype(jnp.float32)
            ).astype(relay.dtype)

        @pl.when(me < n_tp - 1)
        def _():
            left_copy(me, c).wait_recv()
            relay[c] = (
                relay[c].astype(jnp.float32) + left_in[me, c].astype(jnp.float32)
            ).astype(relay.dtype)

        relay_copy(c).start()
        return 0

    lax.fori_loop(0, chunks, final_step, 0)

    def drain_step(i, _):
        turn, c = i // chunks, lax.rem(i, chunks)
        far = n_tp - 1 - turn

        @pl.when(far > me)
        def _():
            right_copy(far, c).wait_send()

        @pl.when(turn < me)
        def _():
            left_copy(turn, c).wait_send()

        return 0

    lax.fori_loop(0, (n_tp - 1) * chunks, drain_step, 0)

    def relay_step(c, _):
        relay_copy(c).wait_send()
        relay_copy(c).wait_recv()
        return 0

    lax.fori_loop(0, chunks, relay_step, 0)
    for copy in part_sent:
        copy.wait_send()


def per_device(
    n_tp, n_ctx, n_sec, stretch_order, queries, key_rows, value_rows, out_grad,
    query_weight, key_weight, value_weight, output_weight,
):
    tok, q_cols = queries.shape[1:]
    rows, width = out_grad.shape[1:]
    seq = tok * n_ctx
    low = jnp.bfloat16
    dma = pltpu.SemaphoreType.DMA
    chunks = width // CHUNK
    attn_grad, keys_all, values_all = pl.pallas_call(
        functools.partial(gather_kernel, n_tp, n_ctx),
        out_shape=(
            jax.ShapeDtypeStruct((tok, q_cols), low),
            jax.ShapeDtypeStruct((seq, HD), low),
            jax.ShapeDtypeStruct((seq, HD), low),
        ),
        in_specs=[VMEM] * 4,
        out_specs=(VMEM,) * 3,
        scratch_shapes=[
            pltpu.VMEM((n_tp - 1, rows, width), low),
            dma((n_tp - 1,)), dma((n_tp - 1,)),
            dma((2, n_ctx - 1)), dma((2, n_ctx - 1)),
        ],
        compiler_params=pltpu.CompilerParams(
            collective_id=0, has_side_effects=True, vmem_limit_bytes=LIMIT
        ),
    )(out_grad[0], output_weight[0], key_rows[0], value_rows[0])
    query_grad, kv_parts = pl.pallas_call(
        attention_kernel,
        out_shape=(
            jax.ShapeDtypeStruct((tok, q_cols), low),
            jax.ShapeDtypeStruct((2, seq, HD), low),
        ),
        in_specs=[SMEM] + [VMEM] * 4,
        out_specs=(VMEM,) * 2,
        scratch_shapes=[
            pltpu.VMEM((seq, HD), jnp.float32),
            pltpu.VMEM((seq, HD), jnp.float32),
            pltpu.VMEM((HD, seq), low),
        ],
        compiler_params=pltpu.CompilerParams(vmem_limit_bytes=LIMIT),
    )(stretch_order, queries[0], attn_grad, keys_all, values_all)
    travel = pltpu.VMEM((n_tp, chunks, rows, CHUNK), low)
    sent_grad, key_grad, value_grad = pl.pallas_call(
        functools.partial(scatter_kernel, n_tp, n_ctx, n_sec),
        out_shape=(
            jax.ShapeDtypeStruct((rows, width), low),
            jax.ShapeDtypeStruct((tok, HD), low),
            jax.ShapeDtypeStruct((tok, HD), low),
        ),
        in_specs=[VMEM] * 5,
        out_specs=(VMEM,) * 3,
        scratch_shapes=[
            pltpu.VMEM((n_ctx - 1, 2, tok, HD), low),
            travel, travel, travel, travel,
            pltpu.VMEM((chunks, rows, CHUNK), low),
            dma((n_ctx - 1,)), dma((n_ctx - 1,)),
            dma((n_tp, chunks)), dma((n_tp, chunks)),
            dma((n_tp, chunks)), dma((n_tp, chunks)),
            dma((chunks,)), dma((chunks,)),
        ],
        compiler_params=pltpu.CompilerParams(
            collective_id=1, has_side_effects=True, vmem_limit_bytes=LIMIT
        ),
    )(query_grad, kv_parts, query_weight[0], key_weight[0], value_weight[0])
    return (sent_grad[None], key_grad[None], value_grad[None])


def solution(mesh):
    placed = (
        P(),
        P("section", "ctx", "tp"),
        P("section", "ctx", "tp"),
        P("section", "ctx", "tp"),
        P("section", ("ctx", "tp"), None),
        P("section", None, "tp"),
        P("section", None, "tp"),
        P("section", None, "tp"),
        P("section", "tp", None),
    )
    body = functools.partial(
        per_device, mesh.shape["tp"], mesh.shape["ctx"], mesh.shape["section"]
    )
    return jax.shard_map(
        body,
        mesh=mesh,
        in_specs=placed,
        out_specs=(
            P("section", ("ctx", "tp"), None),
            P("section", "ctx", "tp"),
            P("section", "ctx", "tp"),
        ),
        check_vma=False,
    )
```

time: 302 us -> 235 us (0.78); the launches traced: 299 us -> 235 us
  Pallas kernels: 0 us -> 229 us
  waiting for transfers between devices: 163 us -> 0 us
  matrix products: 49.9 us -> 0 us
  other arithmetic: 26.4 us -> 0 us
  between operations: 17.7 us -> 0.65 us
  local copies, waits for them, and re-layouts: 19.2 us -> 5.42 us
  loops' own time: 11.1 us -> 0 us
  blocking collectives: 10 us -> 0 us
    pallas_call x0 -> x3, Pallas kernels: none -> 229 us  [the longest x1 118 us: per_device(): pl.pallas_call(functools.partial(scatter_kernel, n_tp, n_ctx, n_sec), out...]
    reduce_scatter x3 -> x0, waiting for transfers between devices: 89 us -> none  [the longest x1 77 us: per_device(): lax.psum_scatter(summed.astype(jnp.bfloat16), 'tp', scatter_dimension=0,...]
    all_gather x1 -> x0, waiting for transfers between devices: 59.9 us -> none  [per_device(): lax.all_gather(out_grad[0], 'tp', axis=0, tiled=True)]
    dot_general x33 -> x0, matrix products: 49.9 us -> none  [the longest x4 28 us: contract_last(): lax.dot_general(lhs, rhs, (((1,), (1,)), ((), ())), preferred_element_typ...]
    ppermute x1 -> x0, waiting for transfers between devices: 13.8 us -> none  [shifted(): return lax.ppermute(block, axis, route)]
    another operation x11 -> x0, loops' own time: 11.1 us -> none  [the longest x1 10.4 us: per_device(): lax.fori_loop(0, block_total, grad_step, ((zero_query, zero_query), zero_...]
    all_gather x2 -> x0, blocking collectives: 10 us -> none  [the longest x1 5.14 us: per_device(): lax.all_gather(key_mat, 'ctx', axis=0, tiled=True)]
    add x13 -> x0, other arithmetic: 9.05 us -> none  [the longest x4 7.66 us: grad_step(): new_query.append(query_sums[half_idx] + part_query)]
  transfers between devices with their start and end apart: 5 -> 0, of which waited for: 5 -> 0; matrix products, arithmetic and copies ran while one was open for 8% -> 0% of each run, Pallas kernels for 0% -> 0%
where the time goes in v1:
time: 235 us
  Pallas kernels  229 us (97%)
  local copies, waits for them, and re-layouts  5.42 us (2%)
    pallas_call x1, Pallas kernels, per_device(): pl.pallas_call(functools.partial(scatter_kernel, n_tp, n_ctx, n_sec), out...  118 us
    pallas_call x1, Pallas kernels, per_device(): pl.pallas_call(functools.partial(gather_kernel, n_tp, n_ctx), out_shape=(...  97.8 us
    pallas_call x1, Pallas kernels, per_device(): pl.pallas_call(attention_kernel, out_shape=(jax.ShapeDtypeStruct((tok, q_...  12.4 us
    unnamed x3, local copies, waits for them, and re-layouts  5.42 us

profile of v1, /device:TPU:9, one launch (start us, length us, event | category | flops | bytes accessed | tf_op | source)
XLA Modules:
  0.0 234.7 jit_solution(4327497215659026010)
XLA Ops:
  0.6 97.8 %shard_map.112 = (bf16[512,512]{1,0:T(8,128)(2,1)}, bf16[1024,128]{1,0:T(8,128)(2,1)}, bf16[1024,128]{1,0:T(8,128)(2,1)}) custom-call(bf16[128,4096]{1,0:T(8,128)(2,1)} %bitcast.16, bf16[512,4096]{1,0:T(8,128)(2,1)} %bitcast.12, bf16[512,128]{1,0:T(8,128)(2,1)} %bitcast.18, bf16[512,128]{1,0:T(8,128)(2,1)} %bitcast.19), custom_call_target="tpu_custom_call" | custom-call | tf_op jit(solution)/shard_map/pallas_call | solution.py:297
  98.5 12.4 %shard_map.113 = (bf16[512,512]{1,0:T(8,128)(2,1)}, bf16[2,1024,128]{2,1,0:T(8,128)(2,1)}) custom-call(s32[2,2]{1,0:T(2,128)} %order_ref.1, bf16[512,512]{1,0:T(8,128)(2,1)} %bitcast.17, bf16[512,512]{1,0:T(8,128)(2,1)} %get-tuple-element.11.g_ref, bf16[1024,128]{1,0:T(8,128)(2,1)} %get-tuple-element.12.k_ref, bf16[1024,128]{1,0:T(8,128)(2,1)} %get-tuple-element.13.v_ref), custom_call_target="tpu_custom_call" | custom-call | tf_op jit(solution)/shard_map/pallas_call | solution.py:315
  110.9 118.4 %shard_map.114 = (bf16[128,4096]{1,0:T(8,128)(2,1)}, bf16[512,128]{1,0:T(8,128)(2,1)}, bf16[512,128]{1,0:T(8,128)(2,1)}) custom-call(bf16[512,512]{1,0:T(8,128)(2,1)} %get-tuple-element.14.dq_ref, bf16[2,1024,128]{2,1,0:T(8,128)(2,1)} %get-tuple-element.15.dkv_ref, bf16[4096,512]{1,0:T(8,128)(2,1)} %bitcast.11, bf16[4096,128]{1,0:T(8,128)(2,1)} %bitcast.13, ...), custom_call_target="tpu_custom_call" | custom-call | tf_op jit(solution)/shard_map/pallas_call | solution.py:331
  229.3 2.3 copy.15
  231.5 1.6 copy.16
  233.1 1.6 copy.17

commit v2 on v1

--- a/solution.py
+++ b/solution.py
@@ -12,6 +12,8 @@
 MASKED = -1e30
 LOG2E = 1.4426950408889634
 CHUNK = 512
+PIECE = 32
+LAG = 3
 MESH = pl.DeviceIdType.MESH
 VMEM = pl.BlockSpec(memory_space=pltpu.VMEM)
 SMEM = pl.BlockSpec(memory_space=pltpu.SMEM)
@@ -45,15 +47,29 @@
         [{"tp": lax.rem(me + i, n_tp)} for i in range(1, n_tp)]
         + [{"ctx": lax.rem(ctx + i, n_ctx)} for i in range(1, n_ctx)]
     )
-    sent = []
-    for i in range(1, n_tp):
-        copy = pltpu.make_async_remote_copy(
-            src_ref=og_ref, dst_ref=shards.at[i - 1], send_sem=og_send.at[i - 1],
-            recv_sem=og_recv.at[i - 1], device_id={"tp": lax.rem(me + i, n_tp)},
-            device_id_type=MESH,
-        )
-        copy.start()
-        sent.append(copy)
+    pieces = rows // PIECE
+
+    def hop(which, owner, c, own):
+        at = pl.ds(pl.multiple_of(c * PIECE, PIECE), PIECE)
+        step = n_tp - 1 if which else 1
+        return pltpu.make_async_remote_copy(
+            src_ref=og_ref.at[at] if own else shards.at[owner, at],
+            dst_ref=shards.at[owner, at], send_sem=og_send.at[which, owner, c],
+            recv_sem=og_recv.at[which, owner, c],
+            device_id={"tp": lax.rem(me + step, n_tp)}, device_id_type=MESH,
+        )
+
+    def own_step(c, _):
+        @pl.when(me < n_tp - 1)
+        def _():
+            hop(0, me, c, True).start()
+
+        @pl.when(me > 0)
+        def _():
+            hop(1, me, c, True).start()
+
+        return 0
+
     place = pl.ds(pl.multiple_of(ctx * tok, tok), tok)
     kv_sent = []
     for i in range(1, n_ctx):
@@ -65,6 +81,7 @@
             )
             copy.start()
             kv_sent.append(copy)
+    lax.fori_loop(0, pieces, own_step, 0)
     kall_ref[place, :] = k_ref[...]
     vall_ref[place, :] = v_ref[...]
 
@@ -73,9 +90,36 @@
         grad_ref[at, :] = dot_nt(block[...], wo_ref[...]).astype(grad_ref.dtype)
 
     store(me, og_ref)
-    for i in range(1, n_tp):
-        sent[i - 1].wait_recv()
-        store(lax.rem(me - i + n_tp, n_tp), shards.at[i - 1])
+    for d in range(1, n_tp):
+        def pass_on(c, _):
+            @pl.when(me >= d)
+            def _():
+                hop(0, me - d, c, False).wait_recv()
+
+                @pl.when(me < n_tp - 1)
+                def _():
+                    hop(0, me - d, c, False).start()
+
+            @pl.when(me + d < n_tp)
+            def _():
+                hop(1, me + d, c, False).wait_recv()
+
+                @pl.when(me > 0)
+                def _():
+                    hop(1, me + d, c, False).start()
+
+            return 0
+
+        lax.fori_loop(0, pieces, pass_on, 0)
+
+        @pl.when(me >= d)
+        def _():
+            store(me - d, shards.at[me - d])
+
+        @pl.when(me + d < n_tp)
+        def _():
+            store(me + d, shards.at[me + d])
+
     for i in range(1, n_ctx):
         source = lax.rem(ctx - i + n_ctx, n_ctx)
         at = pl.ds(pl.multiple_of(source * tok, tok), tok)
@@ -85,8 +129,23 @@
                 recv_sem=kv_recv.at[which, i - 1], device_id={"ctx": lax.rem(ctx + i, n_ctx)},
                 device_id_type=MESH,
             ).wait_recv()
-    for copy in sent + kv_sent:
+    for copy in kv_sent:
         copy.wait_send()
+
+    def drained(i, _):
+        owner, c = i // pieces, lax.rem(i, pieces)
+
+        @pl.when((owner <= me) & (me < n_tp - 1))
+        def _():
+            hop(0, owner, c, False).wait_send()
+
+        @pl.when((owner >= me) & (me > 0))
+        def _():
+            hop(1, owner, c, False).wait_send()
+
+        return 0
+
+    lax.fori_loop(0, n_tp * pieces, drained, 0)
 
 
 def attention_kernel(
@@ -220,21 +279,30 @@
 
         make(block, c).start()
 
+    right_total = (n_tp - 1 - me) * chunks
+    left_total = me * chunks
+    left_lag = jnp.where(2 * me < n_tp, LAG, 0)
+    right_lag = LAG - left_lag
+
     def forward_step(i, _):
-        turn, c = i // chunks, lax.rem(i, chunks)
-        far = n_tp - 1 - turn
-
-        @pl.when(far > me)
-        def _():
-            forward(right_copy, right_in, right_out, me > 0, far, c)
-
-        @pl.when(turn < me)
-        def _():
-            forward(left_copy, left_in, left_out, me < n_tp - 1, turn, c)
-
-        return 0
-
-    lax.fori_loop(0, (n_tp - 1) * chunks, forward_step, 0)
+        r = i - right_lag
+        l = i - left_lag
+
+        @pl.when((2 * me < n_tp) & (r < right_total))
+        def _():
+            forward(right_copy, right_in, right_out, me > 0, n_tp - 1 - r // chunks, lax.rem(r, chunks))
+
+        @pl.when((l >= 0) & (l < left_total))
+        def _():
+            forward(left_copy, left_in, left_out, me < n_tp - 1, l // chunks, lax.rem(l, chunks))
+
+        @pl.when((2 * me >= n_tp) & (r >= 0) & (r < right_total))
+        def _():
+            forward(right_copy, right_in, right_out, me > 0, n_tp - 1 - r // chunks, lax.rem(r, chunks))
+
+        return 0
+
+    lax.fori_loop(0, (n_tp - 1) * chunks + LAG, forward_step, 0)
 
     def final_step(c, _):
         relay[c] = term(me, c).astype(relay.dtype)
@@ -304,8 +372,8 @@
         in_specs=[VMEM] * 4,
         out_specs=(VMEM,) * 3,
         scratch_shapes=[
-            pltpu.VMEM((n_tp - 1, rows, width), low),
-            dma((n_tp - 1,)), dma((n_tp - 1,)),
+            pltpu.VMEM((n_tp, rows, width), low),
+            dma((2, n_tp, rows // PIECE)), dma((2, n_tp, rows // PIECE)),
             dma((2, n_ctx - 1)), dma((2, n_ctx - 1)),
         ],
         compiler_params=pltpu.CompilerParams(

time: 235 us -> 184 us (0.78)
  Pallas kernels: 229 us -> 177 us
    pallas_call x1, Pallas kernels: 118 us -> 91 us  [per_device(): pl.pallas_call(functools.partial(scatter_kernel, n_tp, n_ctx, n_sec), out...]
    pallas_call x1, Pallas kernels: 97.8 us -> 73.2 us  [per_device(): pl.pallas_call(functools.partial(gather_kernel, n_tp, n_ctx), out_shape=(...]
where the time goes in v2:
time: 184 us; the launch traced here: 183 us
  Pallas kernels  177 us (96%)
  local copies, waits for them, and re-layouts  5.42 us (3%)
    pallas_call x1, Pallas kernels, per_device(): pl.pallas_call(functools.partial(scatter_kernel, n_tp, n_ctx, n_sec), out...  91 us
    pallas_call x1, Pallas kernels, per_device(): pl.pallas_call(functools.partial(gather_kernel, n_tp, n_ctx), out_shape=(...  73.2 us
    pallas_call x1, Pallas kernels, per_device(): pl.pallas_call(attention_kernel, out_shape=(jax.ShapeDtypeStruct((tok, q_...  12.4 us
    unnamed x3, local copies, waits for them, and re-layouts  5.42 us

profile of v2, /device:TPU:9, one launch (start us, length us, event | category | flops | bytes accessed | tf_op | source)
XLA Modules:
  0.0 182.7 jit_solution(10132945175466919475)
XLA Ops:
  0.6 73.2 %shard_map.112 = (bf16[512,512]{1,0:T(8,128)(2,1)}, bf16[1024,128]{1,0:T(8,128)(2,1)}, bf16[1024,128]{1,0:T(8,128)(2,1)}) custom-call(bf16[128,4096]{1,0:T(8,128)(2,1)} %bitcast.16, bf16[512,4096]{1,0:T(8,128)(2,1)} %bitcast.12, bf16[512,128]{1,0:T(8,128)(2,1)} %bitcast.18, bf16[512,128]{1,0:T(8,128)(2,1)} %bitcast.19), custom_call_target="tpu_custom_call" | custom-call | tf_op jit(solution)/shard_map/pallas_call | solution.py:365
  73.8 12.4 %shard_map.113 = (bf16[512,512]{1,0:T(8,128)(2,1)}, bf16[2,1024,128]{2,1,0:T(8,128)(2,1)}) custom-call(s32[2,2]{1,0:T(2,128)} %order_ref.1, bf16[512,512]{1,0:T(8,128)(2,1)} %bitcast.17, bf16[512,512]{1,0:T(8,128)(2,1)} %get-tuple-element.11.g_ref, bf16[1024,128]{1,0:T(8,128)(2,1)} %get-tuple-element.12.k_ref, bf16[1024,128]{1,0:T(8,128)(2,1)} %get-tuple-element.13.v_ref), custom_call_target="tpu_custom_call" | custom-call | tf_op jit(solution)/shard_map/pallas_call | solution.py:383
  86.2 91.0 %shard_map.114 = (bf16[128,4096]{1,0:T(8,128)(2,1)}, bf16[512,128]{1,0:T(8,128)(2,1)}, bf16[512,128]{1,0:T(8,128)(2,1)}) custom-call(bf16[512,512]{1,0:T(8,128)(2,1)} %get-tuple-element.14.dq_ref, bf16[2,1024,128]{2,1,0:T(8,128)(2,1)} %get-tuple-element.15.dkv_ref, bf16[4096,512]{1,0:T(8,128)(2,1)} %bitcast.11, bf16[4096,128]{1,0:T(8,128)(2,1)} %bitcast.13, ...), custom_call_target="tpu_custom_call" | custom-call | tf_op jit(solution)/shard_map/pallas_call | solution.py:399
  177.3 2.3 %copy.15 = bf16[1,128,4096]{2,1,0:T(8,128)(2,1)} copy(bf16[1,128,4096]{2,1,0:T(8,128)(2,1)} %bitcast.15) | data formatting | bytes 2097152
  179.6 1.6 copy.16
  181.1 1.6 copy.17
